TPU v7x, 32 devices: a whole 2x2x4 slice. The times are simulated.
32 devices in a mesh: groups: 2 (over x), bricks: 16 (over z, y, core).
Axes of the slice: x: 2, y: 2, z: 4, core: 2. Of those that a mesh axis runs over, the one named last changes fastest.
Arguments:
- features: bfloat16 [16384, 128], P(('groups', 'bricks')), parts along dimension 0, may hold values from -6 to 6
- conv_weight: bfloat16 [27, 128, 128], replicated, may hold values from -0.109375 to 0.109375
- in_projection: bfloat16 [128, 384], replicated, may hold values from -0.5 to 0.5
- out_projection: bfloat16 [128, 128], replicated, may hold values from -0.5 to 0.5
- head_scale: float32 [2], replicated, may hold values from 3 to 20
- neighbours: int32 [27, 16384], P(None, ('groups', 'bricks')), parts along dimension 1, may hold values from 0 to 640, as said below
- send_rows: int32 [64, 64], P(('groups', 'bricks')), parts along dimension 0, may hold values from 0 to 511, as said below
- send_count: int32 [64], P(('groups', 'bricks')), parts along dimension 0, may hold values from 32 to 64
- window_slot: int32 [16384], P(('groups', 'bricks')), parts along dimension 0, may hold values from 0 to 8191, as said below
- cotangent: bfloat16 [16384, 128], P(('groups', 'bricks')), parts along dimension 0, may hold values from -6 to 6
Outputs:
- mixed: bfloat16 [16384, 128], P(('groups', 'bricks')), parts along dimension 0
- grad_features: bfloat16 [16384, 128], P(('groups', 'bricks')), parts along dimension 0
- grad_conv: float32 [54, 128, 128], P('groups'), parts along dimension 0
- grad_in_projection: float32 [256, 384], P('groups'), parts along dimension 0
- grad_out_projection: float32 [256, 128], P('groups'), parts along dimension 0
There are 2 independent parts, one for each index of `groups`. A program takes and returns all parts, laid end to end along the dimension named above; an argument that names none is the same for every part. Nothing has to cross between parts.
Inputs may be any that keep to these rules, and one draw needn't show every extreme that they name: `neighbours`: in column b * 512 + v: a value below 512 is a voxel of brick b; 512 + j with j below brick b-1's count send_count[2b-1] and 576 + j with j below send_count[2b+2] name received slots; 640 means no neighbour, and is used for every slot of a missing neighbouring brick; offset 27 // 2 names the voxel itself. `send_rows`: each row holds distinct local rows. `window_slot`: A permutation; each brick sends at most 48 of its voxels into the 512 consecutive positions of any one brick, and exactly 48 into some.
All inputs are finite; a program needn't handle non-finite values.
Results may differ from a plain program's by a relative error of at most 0.015.
Values may be sent and summed in bfloat16 or wider, within the bound.
A program may use at most 64 MiB of HBM per device.

v0:
```python
import functools

import jax
import jax.numpy as jnp
from jax import lax
from jax.experimental import pallas as pl
from jax.experimental.pallas import tpu as pltpu
from jax.sharding import PartitionSpec as P

HEADS = 2
EPS = 1e-06
F32 = jnp.float32
BF16 = jnp.bfloat16
VMEM = pl.BlockSpec(memory_space=pltpu.VMEM)
SMEM = pl.BlockSpec(memory_space=pltpu.SMEM)


def dot(a, b, ca=1, cb=0):
    return lax.dot_general(a, b, (((ca,), (cb,)), ((), ())), preferred_element_type=F32)


def iota(shape, dim):
    return lax.broadcasted_iota(jnp.int32, shape, dim)


def select_rows(rows, lane_index):
    shape = (rows, lane_index.shape[1])
    return jnp.where(iota(shape, 0) == lane_index, 1.0, 0.0).astype(BF16)


def rank_plan(slot, devices, cap):
    height = slot.shape[1]
    bits = height.bit_length() - 1
    target = lax.shift_right_logical(slot, jnp.full_like(slot, bits))
    within = slot & (height - 1)
    member = iota((devices, height), 0) == target
    before = jnp.where(iota((height, height), 0) < iota((height, height), 1), 1.0, 0.0).astype(BF16)
    ones = jnp.where(member, 1.0, 0.0)
    counts = dot(ones.astype(BF16), before)
    rank = jnp.sum(counts * ones, axis=0, keepdims=True).astype(jnp.int32)
    return target, within, rank, target * cap + rank


def position_rows(target, within, rank, me, devices, cap):
    slots = devices * cap
    height = target.shape[1]
    where_to = select_rows(slots, rank + me * cap)
    shown = within + 1
    hit = iota((devices, height), 0) == target
    high = jnp.where(hit, lax.shift_right_logical(shown, jnp.full_like(shown, 8)), 0)
    low = jnp.where(hit, shown & 255, 0)
    return (
        dot(high.astype(F32).astype(BF16), where_to, 1, 1),
        dot(low.astype(F32).astype(BF16), where_to, 1, 1),
    )


def border_select(send, count0, count1, height):
    both = send.shape[1]
    lane = iota((1, both), 1)
    limit = jnp.where(lane < both // 2, count0, count1 + both // 2)
    return select_rows(height, jnp.where(lane < limit, send, -1))


def attention(win, grad_win, in_proj, out_proj, scale):
    width = win.shape[1]
    dim = width // HEADS
    projected = dot(in_proj, win, 0, 1).astype(BF16).astype(F32)
    grad_core = dot(out_proj, grad_win, 1, 1).astype(BF16)
    cores, grads = [], [[], [], []]
    for h in range(HEADS):
        q = projected[h * dim : (h + 1) * dim]
        k = projected[width + h * dim : width + (h + 1) * dim]
        v = projected[2 * width + h * dim : 2 * width + (h + 1) * dim].astype(BF16)
        rq = lax.rsqrt(jnp.sum(q * q, axis=0, keepdims=True) + EPS)
        rk = lax.rsqrt(jnp.sum(k * k, axis=0, keepdims=True) + EPS)
        qp = (q * rq * scale[h]).astype(BF16)
        kp = (k * rk).astype(BF16)
        grad_h = grad_core[h * dim : (h + 1) * dim]
        e = jnp.exp(dot(kp, qp, 0, 0))
        p = e * (1.0 / jnp.sum(e, axis=0, keepdims=True))
        w = p.astype(BF16)
        cores.append(dot(v, w).astype(BF16))
        dw = dot(v, grad_h, 0, 0).astype(BF16).astype(F32)
        dv = dot(grad_h, w, 1, 1)
        ds = (p * (dw - jnp.sum(dw * p, axis=0, keepdims=True))).astype(BF16)
        dqp = dot(kp, ds).astype(BF16).astype(F32)
        dkp = dot(qp, ds, 1, 1).astype(BF16).astype(F32)
        dq = scale[h] * rq * (dqp - q * (rq * rq) * jnp.sum(dqp * q, axis=0, keepdims=True))
        dk = rk * (dkp - k * (rk * rk) * jnp.sum(dkp * k, axis=0, keepdims=True))
        grads[0].append(dq.astype(BF16))
        grads[1].append(dk.astype(BF16))
        grads[2].append(dv.astype(BF16))
    core = jnp.concatenate(cores, axis=0)
    grad_projected = jnp.concatenate(grads[0] + grads[1] + grads[2], axis=0)
    mixed = dot(out_proj, core, 0, 0).astype(BF16)
    grad_back = dot(in_proj, grad_projected).astype(BF16)
    grad_in = dot(win, grad_projected, 0, 1)
    grad_out = dot(core, grad_win)
    return mixed, grad_back, grad_in, grad_out


def start_kernel(devices, cap, halo, feat, cot, slot, send, count, place, message, border, stage):
    me = lax.axis_index("bricks")
    height = feat.shape[0]
    slots = devices * cap
    target, within, rank, placing = rank_plan(slot[...], devices, cap)
    place[...] = placing
    chosen = border_select(send[...], count[0], count[1], height)
    border[...] = dot(chosen, feat[...], 0, 0).astype(BF16)
    rows = dot(select_rows(slots, placing), cot[...])
    message[:, :cap, :] = rows.astype(BF16).reshape(devices, cap, -1)
    high, low = position_rows(target, within, rank, me, devices, cap)
    stage[...] = jnp.zeros_like(stage)
    chunks = slots // 128
    for r in range(chunks):
        stage[:, r, :] = high[:, r * 128 : (r + 1) * 128]
        stage[:, chunks + r, :] = low[:, r * 128 : (r + 1) * 128]
    message[:, cap:, :] = stage[...].astype(BF16)


def conv_kernel(feat, halo, near, weight, slot, filtered, sent, gathered, table):
    height, width = feat.shape
    offsets = near.shape[0]
    slots = sent.shape[0]
    both = jnp.concatenate([feat[...], halo[...]], axis=0)
    table[...] = both.astype(F32).T.astype(BF16)

    def step(k, carry):
        chosen = select_rows(both.shape[0], near[pl.ds(k, 1), :])
        at = pl.ds(pl.multiple_of(k * width, width), width)
        gathered[at, :] = dot(table[...], chosen).astype(BF16)
        return carry

    lax.fori_loop(0, offsets, step, 0)
    total = dot(weight[...], gathered[...], 0, 0)
    filtered[...] = total
    activated = (total * jax.nn.sigmoid(total)).astype(BF16)
    sent[...] = dot(activated, select_rows(slots, slot[...]), 1, 1).T.astype(BF16)


def window_call(cap, act, cot, in_proj, out_proj, scale, mixed_out, grad_back_out, grad_in, grad_out, height):
    devices = cot.shape[0]
    slots = devices * cap
    chunks = slots // 128
    marks = jnp.sum(cot[:, cap:, :].astype(F32), axis=0)
    landing = jnp.concatenate(
        [marks[r : r + 1] * 256.0 + marks[chunks + r : chunks + r + 1] for r in range(chunks)], axis=1
    ).astype(jnp.int32) - 1
    chosen = select_rows(height, landing)
    win = dot(chosen, act[...]).astype(BF16)
    grad_win = dot(chosen, cot[:, :cap, :].reshape(slots, -1)).astype(BF16)
    mixed, grad_back, grad_i, grad_o = attention(
        win, grad_win, in_proj[...], out_proj[...], (scale[0], scale[1])
    )
    mixed_out[...] = dot(mixed, chosen).T.astype(BF16)
    grad_back_out[...] = dot(grad_back, chosen).T.astype(BF16)
    grad_in[...] = grad_i
    grad_out[...] = grad_o


def brick_kernel(
    height, mixed_in, back_in, place, filtered, gathered, near, weight,
    mixed, kernel_grad, spread, grads,
):
    offsets = near.shape[0]
    width = filtered.shape[0]
    chosen = select_rows(mixed_in.shape[0], place[...])
    mixed[...] = dot(mixed_in[...], chosen, 0, 0).T.astype(BF16)
    grad_act = dot(back_in[...], chosen, 0, 0)
    f = filtered[...]
    sigmoid = jax.nn.sigmoid(f)
    grad = (grad_act * (sigmoid * (1.0 + f * (1.0 - sigmoid)))).T.astype(BF16)
    grads[...] = grad
    kernel_grad[...] = dot(gathered[...], grad)
    spread[...] = jnp.zeros_like(spread)

    def step(k, carry):
        at = pl.ds(pl.multiple_of(k * width, width), width)
        contrib = dot(grads[...], weight[at, :], 1, 1).astype(BF16)
        spread[...] += dot(select_rows(spread.shape[0], near[pl.ds(k, 1), :]), contrib)
        return carry

    lax.fori_loop(0, offsets, step, 0)


def finish_kernel(local, back, send, count, out):
    chosen = border_select(send[...], count[0], count[1], local.shape[0])
    out[...] = (local[...] + dot(chosen, back[...])).astype(BF16)


def shape(dims, kind):
    return jax.ShapeDtypeStruct(dims, kind)


def params():
    return pltpu.CompilerParams(vmem_limit_bytes=48 * 1024 * 1024)


def swap(low, high):
    devices = lax.axis_size("bricks")
    up = [(i, i + 1) for i in range(devices - 1)]
    down = [(j, i) for i, j in up]
    return lax.ppermute(high, "bricks", up), lax.ppermute(low, "bricks", down)


def exchange(array):
    return lax.all_to_all(array, "bricks", split_axis=0, concat_axis=0, tiled=True)


def body(
    features, conv_weight, in_projection, out_projection, head_scale,
    neighbours, send_rows, send_count, window_slot, cotangent,
):
    height, width = features.shape
    halo = send_rows.shape[1]
    offsets = neighbours.shape[0]
    devices = lax.axis_size("bricks")
    capacity = height // devices + height // devices // 2
    cap = -(-capacity // 16) * 16
    slots = devices * cap
    slot = window_slot.reshape(1, height)
    send = send_rows.reshape(1, 2 * halo)
    weight = conv_weight.reshape(offsets * width, width)
    place, message, border = pl.pallas_call(
        functools.partial(start_kernel, devices, cap, halo),
        out_shape=(
            shape((1, height), jnp.int32),
            shape((devices, cap + 16, width), BF16),
            shape((2 * halo, width), BF16),
        ),
        in_specs=[VMEM] * 4 + [SMEM],
        out_specs=[VMEM] * 3,
        scratch_shapes=[pltpu.VMEM((devices, 16, 128), F32)],
        compiler_params=params(),
    )(features, cotangent, slot, send, send_count)
    cot = exchange(message)
    lower, upper = swap(border[:halo], border[halo:])
    filtered, sent, gathered = pl.pallas_call(
        conv_kernel,
        out_shape=(
            shape((width, height), F32),
            shape((slots, width), BF16),
            shape((offsets * width, height), BF16),
        ),
        in_specs=[VMEM] * 5,
        out_specs=[VMEM] * 3,
        scratch_shapes=[pltpu.VMEM((width, height + 2 * halo), BF16)],
        compiler_params=params(),
    )(features, jnp.concatenate([lower, upper], axis=0), neighbours, weight, place)
    act = exchange(sent.reshape(devices, cap, width)).reshape(slots, width)

    def window(*refs):
        window_call(cap, *refs, height=height)

    mixed_back, grad_back, grad_in, grad_out = pl.pallas_call(
        window,
        out_shape=(
            shape((slots, width), BF16),
            shape((slots, width), BF16),
            shape(in_projection.shape, F32),
            shape(out_projection.shape, F32),
        ),
        in_specs=[VMEM] * 4 + [SMEM],
        out_specs=[VMEM] * 4,
        compiler_params=params(),
    )(act, cot, in_projection, out_projection, head_scale)
    grad_back = exchange(grad_back.reshape(devices, cap, width)).reshape(slots, width)
    mixed_back = exchange(mixed_back.reshape(devices, cap, width)).reshape(slots, width)
    mixed, kernel_grad, spread = pl.pallas_call(
        functools.partial(brick_kernel, height),
        out_shape=(
            shape((height, width), BF16),
            shape((offsets * width, width), F32),
            shape((height + 2 * halo, width), F32),
        ),
        in_specs=[VMEM] * 7,
        out_specs=[VMEM] * 3,
        scratch_shapes=[pltpu.VMEM((height, width), BF16)],
        compiler_params=params(),
    )(mixed_back, grad_back, place, filtered, gathered, neighbours, weight)
    totals = lax.psum((kernel_grad, grad_in, grad_out), "bricks")
    edge = spread[height:].astype(BF16)
    low_back, high_back = swap(edge[:halo], edge[halo:])
    grad_features = pl.pallas_call(
        finish_kernel,
        out_shape=shape((height, width), BF16),
        in_specs=[VMEM] * 3 + [SMEM],
        out_specs=VMEM,
        compiler_params=params(),
    )(spread[:height], jnp.concatenate([low_back, high_back], axis=0), send, send_count)
    factor = (height * devices) ** (-0.5)
    return (
        mixed,
        grad_features,
        totals[0].reshape(conv_weight.shape) * factor,
        totals[1] * factor,
        totals[2] * factor,
    )


def solution(mesh):
    return jax.shard_map(
        body,
        mesh=mesh,
        in_specs=(
            P(("groups", "bricks"), None),
            P(),
            P(),
            P(),
            P(),
            P(None, ("groups", "bricks")),
            P(("groups", "bricks"), None),
            P(("groups", "bricks")),
            P(("groups", "bricks")),
            P(("groups", "bricks"), None),
        ),
        out_specs=(
            P(("groups", "bricks"), None),
            P(("groups", "bricks"), None),
            P("groups", None, None),
            P("groups", None),
            P("groups", None),
        ),
        check_vma=False,
    )
```

profile of v0, /device:TPU:0, one launch (start us, length us, event | category | flops | bytes accessed | tf_op | source)
XLA Modules:
  0.0 215.2 jit_solution(299877695294920389)
XLA Ops:
  7.2 0.0 copy-start.12
  7.2 0.0 all-reduce.3.cloned.1.call-start
  7.2 0.8 reshape.41.send
  8.0 0.0 copy-start.3
  8.0 0.9 copy-done.3
  8.9 0.0 copy-start.6
  8.9 0.9 copy-done.6
  9.8 0.0 copy-start.9
  9.8 0.7 copy-done.9
  10.5 0.0 copy-start.10
  10.5 0.7 copy-done.10
  11.1 0.0 copy-start.7
  11.1 0.0 copy-start.8
  11.1 1.5 shard_map.137
  12.7 0.0 copy-start.5
  12.7 2.5 %collective-permute-start = (bf16[64,128]{1,0:T(8,128)(2,1)S(1)}, bf16[64,128]{1,0:T(8,128)(2,1)S(1)}, u32[]{:S(2)}, u32[]{:S(2)}) collective-permute-start(bf16[64,128]{1,0:T(8,128)(2,1)S(1)} %get-tuple-element.36), channel_id=1, source_target_pairs={{0,1},{1,2},{2,3},{3,4},{4,5},{5,6},{6,7},{7,8},{8,9},{9,10},{10,1... | collective-permute-start | bytes 49160 | tf_op jit(solution)/shard_map/ppermute | solution.py:204
  15.2 1.3 collective-permute-start.1
  16.5 0.0 collective-permute-done
  16.5 3.9 %collective-permute-done.1 = bf16[64,128]{1,0:T(8,128)(2,1)S(1)} collective-permute-done((bf16[64,128]{1,0:T(8,128)(2,1)S(1)}, bf16[64,128]{1,0:T(8,128)(2,1)S(1)}, u32[]{:S(2)}, u32[]{:S(2)}) %collective-permute-start.1) | collective-permute-done | bytes 16416 | tf_op jit(solution)/shard_map/ppermute | solution.py:204
  20.4 1.2 copy-done.1
  21.6 0.8 copy-done.4
  22.4 8.6 %shard_map.138 = (f32[128,512]{1,0:T(8,128)S(1)}, bf16[768,128]{1,0:T(8,128)(2,1)S(1)}, bf16[3456,512]{1,0:T(8,128)(2,1)S(1)}) custom-call(bf16[512,128]{1,0:T(8,128)(2,1)S(1)} %copy-done.3, bf16[128,128]{1,0:T(8,128)(2,1)S(1)} %pad_maximum_fusion.halo, s32[27,512]{1,0:T(8,128)S(1)} %copy-done.4, bf16[3456,128]{1,0:T(8,128)(2,1)S(1)} %bitcast.9, ...), custom_call_target="tpu_custom_call" | custom-call | tf_op jit(solution)/shard_map/pallas_call | solution.py:239
  31.0 0.0 copy-start
  31.0 1.7 copy-done
  32.8 16.7 %all_to_all.20 = bf16[16,48,128]{2,1,0:T(8,128)(2,1)S(1)} all-to-all(bf16[16,48,128]{2,1,0:T(8,128)(2,1)S(1)} %bitcast.16), channel_id=1, replica_groups=mesh['groups'=2,'bricks'=16] {'bricks'}, dimensions={0} | all-to-all | bytes 393216 | tf_op jit(solution)/shard_map/all_to_all | solution.py:208
  49.5 12.6 %all_to_all.21.refs_1_ = bf16[16,64,128]{2,1,0:T(8,128)(2,1)S(1)} all-to-all(bf16[16,64,128]{2,1,0:T(8,128)(2,1)S(1)} %get-tuple-element.21), channel_id=1, replica_groups=mesh['groups'=2,'bricks'=16] {'bricks'}, dimensions={0} | all-to-all | bytes 524288 | tf_op jit(solution)/shard_map/all_to_all | solution.py:208
  62.1 0.0 copy-done.12
  62.1 0.0 copy-done.7
  62.1 0.0 copy-done.8
  62.1 4.6 %shard_map.139 = (bf16[768,128]{1,0:T(8,128)(2,1)S(1)}, bf16[768,128]{1,0:T(8,128)(2,1)S(1)}, f32[128,384]{1,0:T(8,128)}, f32[128,128]{1,0:T(8,128)}) custom-call(bf16[768,128]{1,0:T(8,128)(2,1)S(1)} %bitcast.13, bf16[16,64,128]{2,1,0:T(8,128)(2,1)S(1)} %all_to_all.21.refs_1_, bf16[128,384]{1,0:T(8,128)(2,1)S(1)} %copy-done.7, ...), custom_call_target="tpu_custom_call" | custom-call | tf_op jit(solution)/shard_map/pallas_call | solution.py:256
  66.7 11.7 %all_to_all.22 = bf16[16,48,128]{2,1,0:T(8,128)(2,1)S(1)} all-to-all(bf16[16,48,128]{2,1,0:T(8,128)(2,1)S(1)} %bitcast.15), channel_id=1, replica_groups=mesh['groups'=2,'bricks'=16] {'bricks'}, dimensions={0} | all-to-all | bytes 393216 | tf_op jit(solution)/shard_map/all_to_all | solution.py:208
  78.4 11.6 %all_to_all.23 = bf16[16,48,128]{2,1,0:T(8,128)(2,1)S(1)} all-to-all(bf16[16,48,128]{2,1,0:T(8,128)(2,1)S(1)} %bitcast.14), channel_id=1, replica_groups=mesh['groups'=2,'bricks'=16] {'bricks'}, dimensions={0} | all-to-all | bytes 393216 | tf_op jit(solution)/shard_map/all_to_all | solution.py:208
  90.0 0.0 copy-done.5
  90.0 0.0 copy-done.2
  90.0 17.8 %shard_map.140 = (bf16[512,128]{1,0:T(8,128)(2,1)}, f32[3456,128]{1,0:T(8,128)}, f32[640,128]{1,0:T(8,128)S(1)}) custom-call(bf16[768,128]{1,0:T(8,128)(2,1)S(1)} %bitcast.12, bf16[768,128]{1,0:T(8,128)(2,1)S(1)} %bitcast.11, s32[1,512]{1,0:T(1,128)S(1)} %get-tuple-element.19.slot.place, f32[128,512]{1,0:T(8,128)S(1)} %get-tuple-element.24.filtered, ...), custom_call_target="tpu_custom_call" | custom-call | tf_op jit(solution)/shard_map/pallas_call | solution.py:270
  107.8 0.0 all-reduce.3.cloned.1.call-update
  107.9 1.3 collective-permute-start.2
  109.2 1.3 collective-permute-start.3
  110.5 0.0 collective-permute-done.2
  110.5 1.7 collective-permute-done.3
  112.3 0.0 copy-done.11
  112.3 1.4 shard_map.141
  113.6 90.5 %all-reduce.3.cloned.1.call-done = (f32[3456,128]{1,0:T(8,128)}, f32[128,384]{1,0:T(8,128)}, f32[128,128]{1,0:T(8,128)}) async-done(((f32[3456,128]{1,0:T(8,128)}, f32[128,384]{1,0:T(8,128)}, f32[128,128]{1,0:T(8,128)}), (f32[3456,128]{1,0:T(8,128)}, f32[128,384]{1,0:T(8,128)}, f32[128,128]{1,0:T(8,128)})) %all-reduce.3.cloned.1.call-update) | async-done | bytes 2031632 | tf_op jit(solution)/shard_map/psum | solution.py:282
  204.1 2.9 %broadcast_multiply_fusion = f32[3456,128]{1,0:T(8,128)} fusion(f32[3456,128]{1,0:T(8,128)} %get-tuple-element.31), kind=kLoop, calls=%fused_computation | loop fusion | flops 442368 | bytes 3538944 | tf_op jit(solution)/shard_map/mul | solution.py:296
  207.0 0.0 copy-done.14
  207.0 0.6 broadcast_multiply_fusion.2
  207.6 0.0 copy-done.13
  207.6 0.7 broadcast_multiply_fusion.1
  (12 shorter events, 0.1 us)
Async XLA Ops:
  7.2 54.9 %copy-start.12 = (f32[2]{0:T(128)S(1)}, f32[2]{0:T(128)}, u32[]{:S(2)}) copy-start(f32[2]{0:T(128)} %refs_4_.1) | copy-start | bytes 28
  7.2 196.9 %all-reduce.3.cloned.1.call-start = ((), (), s32[]{:S(2)}) async-start(), calls=%async_computation.4 | async-start | bytes 4063232 | tf_op jit(solution)/shard_map/psum | solution.py:282
  8.0 0.9 copy-start.3
  8.9 0.9 copy-start.6
  9.8 0.7 copy-start.9
  10.5 0.7 copy-start.10
  11.1 51.0 %copy-start.7 = (bf16[128,384]{1,0:T(8,128)(2,1)S(1)}, bf16[128,384]{1,0:T(8,128)(2,1)}, u32[]{:S(2)}) copy-start(bf16[128,384]{1,0:T(8,128)(2,1)} %refs_2_.1) | copy-start | bytes 294916
  11.1 51.0 %copy-start.8 = (bf16[128,128]{1,0:T(8,128)(2,1)S(1)}, bf16[128,128]{1,0:T(8,128)(2,1)}, u32[]{:S(2)}) copy-start(bf16[128,128]{1,0:T(8,128)(2,1)} %refs_3_.1) | copy-start | bytes 98308
  12.7 77.3 %copy-start.5 = (s32[27,512]{1,0:T(8,128)S(1)}, s32[27,512]{1,0:T(8,128)}, u32[]{:S(2)}) copy-start(s32[27,512]{1,0:T(8,128)} %near.3) | copy-start | bytes 165892
  12.7 3.8 %collective-permute-start = (bf16[64,128]{1,0:T(8,128)(2,1)S(1)}, bf16[64,128]{1,0:T(8,128)(2,1)S(1)}, u32[]{:S(2)}, u32[]{:S(2)}) collective-permute-start(bf16[64,128]{1,0:T(8,128)(2,1)S(1)} %get-tuple-element.36), channel_id=1, source_target_pairs={{0,1},{1,2},{2,3},{3,4},{4,5},{5,6},{6,7},{7,8},{8,9},{9,10},{10,1... | collective-permute-start | bytes 49160 | tf_op jit(solution)/shard_map/ppermute | solution.py:204
  15.2 5.2 %collective-permute-start.1 = (bf16[64,128]{1,0:T(8,128)(2,1)S(1)}, bf16[64,128]{1,0:T(8,128)(2,1)S(1)}, u32[]{:S(2)}, u32[]{:S(2)}) collective-permute-start(bf16[64,128]{1,0:T(8,128)(2,1)S(1)} %get-tuple-element.37), channel_id=1, source_target_pairs={{1,0},{2,1},{3,2},{4,3},{5,4},{6,5},{7,6},{8,7},{9,8},{10,9},{11,1... | collective-permute-start | bytes 49160 | tf_op jit(solution)/shard_map/ppermute | solution.py:204
  20.4 1.2 copy-start.1
  21.6 0.8 copy-start.4
  22.4 67.6 %copy-start.2 = (bf16[27,128,128]{2,1,0:T(8,128)(2,1)S(1)}, bf16[27,128,128]{2,1,0:T(8,128)(2,1)}, u32[]{:S(2)}) copy-start(bf16[27,128,128]{2,1,0:T(8,128)(2,1)} %param.11) | copy-start | bytes 2654212
  31.0 1.7 copy-start
  107.8 4.4 %copy-start.11 = (s32[2]{0:T(128)S(1)}, s32[2]{0:T(128)}, u32[]{:S(2)}) copy-start(s32[2]{0:T(128)} %count.3) | copy-start | bytes 28
  107.9 2.6 %collective-permute-start.2 = (bf16[64,128]{1,0:T(8,128)(2,1)S(1)}, bf16[64,128]{1,0:T(8,128)(2,1)S(1)}, u32[]{:S(2)}, u32[]{:S(2)}) collective-permute-start(bf16[64,128]{1,0:T(8,128)(2,1)S(1)} %get-tuple-element.34), channel_id=1, source_target_pairs={{0,1},{1,2},{2,3},{3,4},{4,5},{5,6},{6,7},{7,8},{8,9},{9,10},{10,1... | collective-permute-start | bytes 49160 | tf_op jit(solution)/shard_map/ppermute | solution.py:204
  109.2 3.1 %collective-permute-start.3 = (bf16[64,128]{1,0:T(8,128)(2,1)S(1)}, bf16[64,128]{1,0:T(8,128)(2,1)S(1)}, u32[]{:S(2)}, u32[]{:S(2)}) collective-permute-start(bf16[64,128]{1,0:T(8,128)(2,1)S(1)} %get-tuple-element.35), channel_id=1, source_target_pairs={{1,0},{2,1},{3,2},{4,3},{5,4},{6,5},{7,6},{8,7},{9,8},{10,9},{11,1... | collective-permute-start | bytes 49160 | tf_op jit(solution)/shard_map/ppermute | solution.py:204
  204.1 2.9 %copy-start.14 = (f32[128,128]{1,0:T(8,128)S(1)}, f32[128,128]{1,0:T(8,128)}, u32[]{:S(2)}) copy-start(f32[128,128]{1,0:T(8,128)} %get-tuple-element.33) | copy-start | bytes 196612
  204.1 3.5 %copy-start.13 = (f32[128,384]{1,0:T(8,128)S(1)}, f32[128,384]{1,0:T(8,128)}, u32[]{:S(2)}) copy-start(f32[128,384]{1,0:T(8,128)} %get-tuple-element.32) | copy-start | bytes 589828
Sparse Core Ops, SparseCore 0:
  108.0 96.0 all-reduce.2
where the time goes:
time: 216 us; the launch traced here: 215 us
  waiting for transfers between devices  96.1 us (44%)
  blocking collectives  52.6 us (24%)
  Pallas kernels  33.9 us (16%)
  between operations  14.2 us (7%)
  local copies, waits for them, and re-layouts  7.7 us (4%)
  starting transfers between devices  6.4 us (3%)
  other arithmetic  4.23 us (2%)
    psum x1, waiting for transfers between devices, body(): totals = lax.psum((kernel_grad, grad_in, grad_out), 'bricks')  90.5 us
    all_to_all x4, blocking collectives, exchange(): lax.all_to_all(array, 'bricks', split_axis=0, concat_axis=0, tiled=True)  52.6 us
    pallas_call x1, Pallas kernels, body(): pl.pallas_call(functools.partial(brick_kernel, height), out_shape=(shape(...  17.8 us
    pallas_call x1, Pallas kernels, body(): pl.pallas_call(conv_kernel, out_shape=(shape((width, height), F32), shape...  8.6 us
    unnamed x30, local copies, waits for them, and re-layouts  6.92 us
    ppermute x4, starting transfers between devices, swap(): return (lax.ppermute(high, 'bricks', up), lax.ppermute(low, 'bricks', down))  6.36 us
    ppermute x4, waiting for transfers between devices, swap(): return (lax.ppermute(high, 'bricks', up), lax.ppermute(low, 'bricks', down))  5.65 us
    pallas_call x1, Pallas kernels, body(): pl.pallas_call(window, out_shape=(shape((slots, width), BF16), shape((slo...  4.58 us
  transfers between devices with their start and end apart: 5, of which 3 were waited for; matrix products, arithmetic and copies ran while one was open for 0% of the time, Pallas kernels for 1%

commit v1 on v0

v1 whole, which is shorter than its diff:
```python
import functools

import jax
import jax.numpy as jnp
from jax import lax
from jax.experimental import pallas as pl
from jax.experimental.pallas import tpu as pltpu
from jax.sharding import PartitionSpec as P

HEADS = 2
EPS = 1e-06
F32 = jnp.float32
BF16 = jnp.bfloat16
VMEM = pl.BlockSpec(memory_space=pltpu.VMEM)
SMEM = pl.BlockSpec(memory_space=pltpu.SMEM)


def dot(a, b, ca=1, cb=0):
    return lax.dot_general(a, b, (((ca,), (cb,)), ((), ())), preferred_element_type=F32)


def iota(shape, dim):
    return lax.broadcasted_iota(jnp.int32, shape, dim)


def select_rows(rows, lane_index):
    shape = (rows, lane_index.shape[1])
    return jnp.where(iota(shape, 0) == lane_index, 1.0, 0.0).astype(BF16)


def rank_plan(slot, devices, cap):
    height = slot.shape[1]
    bits = height.bit_length() - 1
    target = lax.shift_right_logical(slot, jnp.full_like(slot, bits))
    within = slot & (height - 1)
    member = iota((devices, height), 0) == target
    before = jnp.where(iota((height, height), 0) < iota((height, height), 1), 1.0, 0.0).astype(BF16)
    ones = jnp.where(member, 1.0, 0.0)
    counts = dot(ones.astype(BF16), before)
    rank = jnp.sum(counts * ones, axis=0, keepdims=True).astype(jnp.int32)
    return target, within, rank, target * cap + rank


def position_rows(target, within, rank, me, devices, cap):
    slots = devices * cap
    height = target.shape[1]
    where_to = select_rows(slots, rank + me * cap)
    shown = within + 1
    hit = iota((devices, height), 0) == target
    high = jnp.where(hit, lax.shift_right_logical(shown, jnp.full_like(shown, 8)), 0)
    low = jnp.where(hit, shown & 255, 0)
    return (
        dot(high.astype(F32).astype(BF16), where_to, 1, 1),
        dot(low.astype(F32).astype(BF16), where_to, 1, 1),
    )


def border_select(send, count0, count1, height):
    both = send.shape[1]
    lane = iota((1, both), 1)
    limit = jnp.where(lane < both // 2, count0, count1 + both // 2)
    return select_rows(height, jnp.where(lane < limit, send, -1))


def heads_forward(projected, scale):
    width = projected.shape[0] // 3
    dim = width // HEADS
    kept = []
    for h in range(HEADS):
        q = projected[h * dim : (h + 1) * dim]
        k = projected[width + h * dim : width + (h + 1) * dim]
        v = projected[2 * width + h * dim : 2 * width + (h + 1) * dim].astype(BF16)
        rq = lax.rsqrt(jnp.sum(q * q, axis=0, keepdims=True) + EPS)
        rk = lax.rsqrt(jnp.sum(k * k, axis=0, keepdims=True) + EPS)
        qp = (q * rq * scale[h]).astype(BF16)
        kp = (k * rk).astype(BF16)
        e = jnp.exp(dot(kp, qp, 0, 0))
        p = e * (1.0 / jnp.sum(e, axis=0, keepdims=True))
        w = p.astype(BF16)
        kept.append((q, k, v, rq, rk, qp, kp, p, w, dot(v, w).astype(BF16)))
    return kept


def heads_backward(kept, grad_core, scale):
    grads = [[], [], []]
    for h in range(HEADS):
        q, k, v, rq, rk, qp, kp, p, w, _ = kept[h]
        dim = q.shape[0]
        grad_h = grad_core[h * dim : (h + 1) * dim]
        dw = dot(v, grad_h, 0, 0).astype(BF16).astype(F32)
        dv = dot(grad_h, w, 1, 1)
        ds = (p * (dw - jnp.sum(dw * p, axis=0, keepdims=True))).astype(BF16)
        dqp = dot(kp, ds).astype(BF16).astype(F32)
        dkp = dot(qp, ds, 1, 1).astype(BF16).astype(F32)
        dq = scale[h] * rq * (dqp - q * (rq * rq) * jnp.sum(dqp * q, axis=0, keepdims=True))
        dk = rk * (dkp - k * (rk * rk) * jnp.sum(dkp * k, axis=0, keepdims=True))
        grads[0].append(dq.astype(BF16))
        grads[1].append(dk.astype(BF16))
        grads[2].append(dv.astype(BF16))
    return jnp.concatenate(grads[0] + grads[1] + grads[2], axis=0)


class Exchange:
    def __init__(self, devices, me, out, into, sems, which):
        self.devices, self.me, self.out, self.into = devices, me, out, into
        self.send, self.recv = sems.at[2 * which], sems.at[2 * which + 1]

    def start(self):
        def step(s, carry):
            to = lax.rem(self.me + s, self.devices)
            pltpu.make_async_remote_copy(
                src_ref=self.out.at[to],
                dst_ref=self.into.at[self.me],
                send_sem=self.send,
                recv_sem=self.recv,
                device_id={"bricks": to},
                device_id_type=pl.DeviceIdType.MESH,
            ).start()
            return carry

        lax.fori_loop(1, self.devices, step, 0)
        self.into[self.me] = self.out[self.me]

    def wait_recv(self):
        part = self.into.at[pl.ds(0, self.devices - 1)]
        pltpu.make_async_copy(part, part, self.recv).wait()

    def wait_send(self):
        part = self.out.at[pl.ds(0, self.devices - 1)]
        pltpu.make_async_copy(part, part, self.send).wait()


class Edges:
    def __init__(self, devices, me, out, into, sems):
        self.has = (me > 0, me < devices - 1)
        self.into = into
        self.copies = [
            pltpu.make_async_remote_copy(
                src_ref=out.at[side],
                dst_ref=into.at[1 - side],
                send_sem=sems.at[side],
                recv_sem=sems.at[2 + 1 - side],
                device_id={"bricks": lax.rem(me + step + devices, devices)},
                device_id_type=pl.DeviceIdType.MESH,
            )
            for side, step in ((0, -1), (1, 1))
        ]

    def blank(self):
        for side in range(2):
            @pl.when(jnp.logical_not(self.has[side]))
            def _():
                self.into[side] = jnp.zeros(self.into.shape[1:], self.into.dtype)

    def start(self):
        for side in range(2):
            @pl.when(self.has[side])
            def _():
                self.copies[side].start()

    def wait(self):
        for side in range(2):
            @pl.when(self.has[side])
            def _():
                self.copies[side].wait_send()
                self.copies[1 - side].wait_recv()


def level_kernel(
    devices, cap, halo, total_rows, factor,
    feat, weight, in_proj, out_proj, near, send, slot, cot, scale, count,
    mixed, grad_features, gathered_grads,
    stage, chosen, gathered, contrib, filtered, local, partial, summed,
    cot_out, cot_in, act_out, act_in, back_out, back_in, mix_out, mix_in,
    halo_out, halo_in, edge_out, edge_in, half_out, half_in,
    sems, halo_sems, edge_sems, half_sems, full_sems,
):
    me = lax.axis_index("bricks")
    height, width = feat.shape
    offsets = near.shape[0]
    slots = devices * cap
    chunks = slots // 128
    table_rows = height + 2 * halo
    barrier = pltpu.get_barrier_semaphore()
    halos = Edges(devices, me, halo_out, halo_in, halo_sems)
    edges = Edges(devices, me, edge_out, edge_in, edge_sems)
    halos.blank()
    edges.blank()

    def greet(s, carry):
        pl.semaphore_signal(
            barrier,
            inc=1,
            device_id={"bricks": lax.rem(me + s, devices)},
            device_id_type=pl.DeviceIdType.MESH,
        )
        return carry

    lax.fori_loop(1, devices, greet, 0)
    cots = Exchange(devices, me, cot_out, cot_in, sems, 0)
    acts = Exchange(devices, me, act_out, act_in, sems, 1)
    backs = Exchange(devices, me, back_out, back_in, sems, 2)
    mixes = Exchange(devices, me, mix_out, mix_in, sems, 3)

    border = border_select(send[...], count[0], count[1], height)
    halo_out[...] = dot(border, feat[...], 0, 0).astype(BF16).reshape(2, halo, width)
    pl.semaphore_wait(barrier, devices - 1)
    halos.start()

    target, within, rank, placing = rank_plan(slot[...], devices, cap)
    to_slots = select_rows(slots, placing)
    cot_out[:, :cap, :] = dot(to_slots, cot[...]).astype(BF16).reshape(devices, cap, width)
    high, low = position_rows(target, within, rank, me, devices, cap)
    stage[...] = jnp.zeros_like(stage)
    for r in range(chunks):
        stage[:, r, :] = high[:, r * 128 : (r + 1) * 128]
        stage[:, chunks + r, :] = low[:, r * 128 : (r + 1) * 128]
    cot_out[:, cap:, :] = stage[...].astype(BF16)
    cots.start()

    def choose(k, carry):
        at = pl.ds(pl.multiple_of(k * height, height), height)
        chosen[:, at] = select_rows(table_rows, near[pl.ds(k, 1), :])
        return carry

    lax.fori_loop(0, offsets, choose, 0)
    halos.wait()
    table = jnp.concatenate(
        [feat[...].astype(F32).T, halo_in[...].reshape(2 * halo, width).astype(F32).T], axis=1
    ).astype(BF16)

    def gather(k, carry):
        at = pl.ds(pl.multiple_of(k * height, height), height)
        rows = pl.ds(pl.multiple_of(k * width, width), width)
        gathered[rows, :] = dot(table, chosen[:, at]).astype(BF16)
        return carry

    lax.fori_loop(0, offsets, gather, 0)
    total = dot(weight[...], gathered[...], 0, 0)
    filtered[...] = total
    activated = (total * jax.nn.sigmoid(total)).astype(BF16)
    act_out[...] = dot(to_slots, activated, 1, 1).astype(BF16).reshape(devices, cap, width)
    acts.start()

    cots.wait_recv()
    marks = jnp.sum(cot_in[:, cap:, :].astype(F32), axis=0)
    landing = jnp.concatenate(
        [marks[r : r + 1] * 256.0 + marks[chunks + r : chunks + r + 1] for r in range(chunks)], axis=1
    ).astype(jnp.int32) - 1
    to_window = select_rows(height, landing)
    grad_win = dot(to_window, cot_in[:, :cap, :].reshape(slots, width)).astype(BF16)
    grad_core = dot(out_proj[...], grad_win, 1, 1).astype(BF16)
    scales = (scale[0], scale[1])
    acts.wait_recv()
    win = dot(to_window, act_in[...].reshape(slots, width)).astype(BF16)
    projected = dot(in_proj[...], win, 0, 1).astype(BF16).astype(F32)
    kept = heads_forward(projected, scales)
    grad_projected = heads_backward(kept, grad_core, scales)
    grad_back = dot(in_proj[...], grad_projected).astype(BF16)
    back_out[...] = dot(grad_back, to_window).T.astype(BF16).reshape(devices, cap, width)
    backs.start()
    core = jnp.concatenate([kept[h][-1] for h in range(HEADS)], axis=0)
    mixed_win = dot(out_proj[...], core, 0, 0).astype(BF16)
    mix_out[...] = dot(mixed_win, to_window).T.astype(BF16).reshape(devices, cap, width)
    base = offsets * width
    grad_in = dot(win, grad_projected, 0, 1)
    parts = in_proj.shape[1] // width
    for j in range(parts):
        partial[base + j * width : base + (j + 1) * width] = grad_in[:, j * width : (j + 1) * width]
    base += parts * width
    partial[base : base + width] = dot(core, grad_win)
    base += width
    partial[base:] = jnp.zeros((total_rows - base, width), F32)

    f = filtered[...]
    sigmoid = jax.nn.sigmoid(f)
    slope = sigmoid * (1.0 + f * (1.0 - sigmoid))
    backs.wait_recv()
    grad_act = dot(back_in[...].reshape(slots, width), to_slots, 0, 0)
    grad = (grad_act * slope).T.astype(BF16)
    partial[: offsets * width] = dot(gathered[...], grad)

    bits = devices.bit_length() - 1
    at, length, offset = 0, total_rows, 0
    places = []

    def halving(b, at, length, offset):
        length = length // 2
        bit = lax.rem(me // (1 << b), 2)
        other = me + (1 - 2 * bit) * (1 << b)
        keep = pl.multiple_of(at + bit * length, 16)
        give = pl.multiple_of(at + (1 - bit) * length, 16)
        half_out[offset : offset + length] = partial[pl.ds(give, length)].astype(BF16)
        copy = pltpu.make_async_remote_copy(
            src_ref=half_out.at[pl.ds(offset, length)],
            dst_ref=half_in.at[pl.ds(offset, length)],
            send_sem=half_sems.at[2 * b],
            recv_sem=half_sems.at[2 * b + 1],
            device_id={"bricks": other},
            device_id_type=pl.DeviceIdType.MESH,
        )
        copy.start()
        return copy, keep, length

    def doubling(b, at, length):
        bit = lax.rem(me // (1 << b), 2)
        other = me + (1 - 2 * bit) * (1 << b)
        part = summed.at[pl.ds(pl.multiple_of(at, 16), length)]
        copy = pltpu.make_async_remote_copy(
            src_ref=part,
            dst_ref=part,
            send_sem=full_sems.at[2 * b],
            recv_sem=full_sems.at[2 * b + 1],
            device_id={"bricks": other},
            device_id_type=pl.DeviceIdType.MESH,
        )
        copy.start()
        return copy

    def contribution(k, carry):
        rows = pl.ds(pl.multiple_of(k * height, height), height)
        taps = pl.ds(pl.multiple_of(k * width, width), width)
        contrib[rows, :] = dot(grad, weight[taps, :], 1, 1).astype(BF16)
        return carry

    def edge_rows():
        lax.fori_loop(0, offsets, contribution, 0)
        edge = dot(chosen[height:, :], contrib[...])
        edge_out[...] = edge.astype(BF16).reshape(2, halo, width)
        edges.start()
        mixes.start()

    def own_rows(piece):
        rows = slice(piece * 128, (piece + 1) * 128)
        local[rows] = dot(chosen[rows, :], contrib[...])

    def take_mixed():
        mixes.wait_recv()
        mixed[...] = dot(mix_in[...].reshape(slots, width), to_slots, 0, 0).T.astype(BF16)

    def finish():
        edges.wait()
        returned = edge_in[...].reshape(2 * halo, width)
        grad_features[...] = (local[...] + dot(border, returned)).astype(BF16)

    work = [edge_rows]
    work += [functools.partial(own_rows, piece) for piece in range(height // 128)]
    work += [take_mixed, finish]

    for b in range(bits):
        copy, at, length = halving(b, at, length, offset)
        places.append((at, length))
        if work:
            work.pop(0)()
        copy.wait()
        partial[pl.ds(at, length)] += half_in[offset : offset + length].astype(F32)
        offset += length
    summed[pl.ds(at, length)] = (partial[pl.ds(at, length)] * factor).astype(BF16)
    for b in reversed(range(bits)):
        at, length = places[b]
        copy = doubling(b, at, length)
        if work:
            work.pop(0)()
        copy.wait()
    for task in work:
        task()
    gathered_grads[...] = summed[...]
    for other in (cots, acts, backs, mixes):
        other.wait_send()


def shape(dims, kind):
    return jax.ShapeDtypeStruct(dims, kind)


def body(
    features, conv_weight, in_projection, out_projection, head_scale,
    neighbours, send_rows, send_count, window_slot, cotangent,
):
    height, width = features.shape
    halo = send_rows.shape[1]
    offsets = neighbours.shape[0]
    devices = lax.axis_size("bricks")
    capacity = height // devices + height // devices // 2
    cap = -(-capacity // 16) * 16
    slots = devices * cap
    parts = in_projection.shape[1] // width
    live = (offsets + parts + 1) * width
    total_rows = -(-live // (16 * devices)) * 16 * devices
    bits = devices.bit_length() - 1
    factor = (height * devices) ** (-0.5)
    rows = pltpu.VMEM((devices, cap, width), BF16)
    marked = pltpu.VMEM((devices, cap + 16, width), BF16)
    pair = pltpu.VMEM((2, halo, width), BF16)
    mixed, grad_features, grads = pl.pallas_call(
        functools.partial(level_kernel, devices, cap, halo, total_rows, factor),
        out_shape=(
            shape((height, width), BF16),
            shape((height, width), BF16),
            shape((total_rows, width), BF16),
        ),
        in_specs=[VMEM] * 8 + [SMEM] * 2,
        out_specs=[VMEM] * 3,
        scratch_shapes=[
            pltpu.VMEM((devices, 16, 128), F32),
            pltpu.VMEM((height + 2 * halo, offsets * height), BF16),
            pltpu.VMEM((offsets * width, height), BF16),
            pltpu.VMEM((offsets * height, width), BF16),
            pltpu.VMEM((width, height), F32),
            pltpu.VMEM((height, width), F32),
            pltpu.VMEM((total_rows, width), F32),
            pltpu.VMEM((total_rows, width), BF16),
            marked, marked, rows, rows, rows, rows, rows, rows,
            pair, pair, pair, pair,
            pltpu.VMEM((total_rows, width), BF16),
            pltpu.VMEM((total_rows, width), BF16),
            pltpu.SemaphoreType.DMA((8,)),
            pltpu.SemaphoreType.DMA((4,)),
            pltpu.SemaphoreType.DMA((4,)),
            pltpu.SemaphoreType.DMA((2 * bits,)),
            pltpu.SemaphoreType.DMA((2 * bits,)),
        ],
        compiler_params=pltpu.CompilerParams(
            collective_id=0, has_side_effects=True, vmem_limit_bytes=56 * 1024 * 1024
        ),
    )(
        features,
        conv_weight.reshape(offsets * width, width),
        in_projection,
        out_projection,
        neighbours,
        send_rows.reshape(1, 2 * halo),
        window_slot.reshape(1, height),
        cotangent,
        head_scale,
        send_count,
    )
    grads = grads.astype(F32).reshape(-1, width, width)
    grad_in = grads[offsets : offsets + parts].transpose(1, 0, 2).reshape(in_projection.shape)
    return (mixed, grad_features, grads[:offsets], grad_in, grads[offsets + parts])


def solution(mesh):
    return jax.shard_map(
        body,
        mesh=mesh,
        in_specs=(
            P(("groups", "bricks"), None),
            P(),
            P(),
            P(),
            P(),
            P(None, ("groups", "bricks")),
            P(("groups", "bricks"), None),
            P(("groups", "bricks")),
            P(("groups", "bricks")),
            P(("groups", "bricks"), None),
        ),
        out_specs=(
            P(("groups", "bricks"), None),
            P(("groups", "bricks"), None),
            P("groups", None, None),
            P("groups", None),
            P("groups", None),
        ),
        check_vma=False,
    )
```

time: 216 us -> 87.4 us (0.40)
  waiting for transfers between devices: 96.1 us -> 0 us
  blocking collectives: 52.6 us -> 0 us
  Pallas kernels: 33.9 us -> 78.6 us
  between operations: 14.2 us -> 0.66 us
  starting transfers between devices: 6.4 us -> 0 us
  other arithmetic: 4.23 us -> 0 us
    psum x1 -> x0, waiting for transfers between devices: 90.5 us -> none  [body(): totals = lax.psum((kernel_grad, grad_in, grad_out), 'bricks')]
    all_to_all x4 -> x0, blocking collectives: 52.6 us -> none  [exchange(): lax.all_to_all(array, 'bricks', split_axis=0, concat_axis=0, tiled=True)]
    pallas_call x5 -> x1, Pallas kernels: 33.9 us -> 78.6 us  [body(): pl.pallas_call(functools.partial(level_kernel, devices, cap, halo, total_...]
    ppermute x4 -> x0, starting transfers between devices: 6.36 us -> none  [swap(): return (lax.ppermute(high, 'bricks', up), lax.ppermute(low, 'bricks', down))]
    ppermute x4 -> x0, waiting for transfers between devices: 5.65 us -> none  [swap(): return (lax.ppermute(high, 'bricks', up), lax.ppermute(low, 'bricks', down))]
    unnamed x30 -> x9, local copies, waits for them, and re-layouts: 6.92 us -> 2.14 us
    mul x3 -> x0, other arithmetic: 4.21 us -> none  [the longest x1 2.88 us: body(): totals[0].reshape(conv_weight.shape) * factor]
    slice x3 -> x4, local copies, waits for them, and re-layouts: 0.03 us -> 3.84 us  [the longest x1 1.48 us: body(): grads[offsets + parts]]
  transfers between devices with their start and end apart: 5 -> 0, of which waited for: 3 -> 0; matrix products, arithmetic and copies ran while one was open for 0% -> 0% of each run, Pallas kernels for 1% -> 0%
where the time goes in v1:
time: 87.4 us; the launch traced here: 86.5 us
  Pallas kernels  78.6 us (90%)
  local copies, waits for them, and re-layouts  7.24 us (8%)
    pallas_call x1, Pallas kernels, body(): pl.pallas_call(functools.partial(level_kernel, devices, cap, halo, total_...  78.6 us
    unnamed x9, local copies, waits for them, and re-layouts  2.14 us

profile of v1, /device:TPU:0, one launch (start us, length us, event | category | flops | bytes accessed | tf_op | source)
XLA Modules:
  0.0 86.5 jit_solution(9136733899399310974)
XLA Ops:
  0.6 1.3 %reshape.28.send = s32[1,128]{1,0:T(1,128)} reshape(s32[2,64]{1,0:T(2,128)} %param.16) | data formatting | bytes 1024 | tf_op jit(solution)/shard_map/reshape | solution.py:432
  1.9 78.6 %shard_map.137 = (bf16[512,128]{1,0:T(8,128)(2,1)}, bf16[512,128]{1,0:T(8,128)(2,1)}, bf16[4096,128]{1,0:T(8,128)(2,1)}) custom-call(bf16[512,128]{1,0:T(8,128)(2,1)} %feat.1, bf16[3456,128]{1,0:T(8,128)(2,1)} %bitcast.8, bf16[128,384]{1,0:T(8,128)(2,1)} %in_proj.1, bf16[128,128]{1,0:T(8,128)(2,1)} %out_proj.1, s32[27,512]{1,0:T(8,128)} %near.1, ...), custom_call_target="tpu_custom_call" | custom-call | tf_op jit(solution)/shard_map/pallas_call | solution.py:395
  80.5 0.0 copy-start
  80.5 1.5 %slice.23 = f32[128,128]{1,0:T(8,128)} slice(bf16[4096,128]{1,0:T(8,128)(2,1)} %get-tuple-element.10), slice={[3840:3968], [0:128]} | slice | bytes 131072 | tf_op jit(solution)/shard_map/slice | solution.py:440
  82.0 0.9 %slice.22 = f32[384,128]{1,0:T(8,128)S(1)} slice(bf16[4096,128]{1,0:T(8,128)(2,1)} %get-tuple-element.10), slice={[3456:3840], [0:128]} | slice | bytes 393216 | tf_op jit(solution)/shard_map/slice | solution.py:439
  82.9 0.1 copy.16
  83.0 0.8 copy.17
  83.8 0.0 copy-done
  83.8 0.0 copy-start.2
  83.8 0.0 copy-start.1
  83.8 1.3 %slice.21 = f32[3456,128]{1,0:T(8,128)} slice(bf16[4096,128]{1,0:T(8,128)(2,1)S(1)} %copy-done), slice={[0:3456], [0:128]} | slice | bytes 3538944 | tf_op jit(solution)/shard_map/slice | solution.py:440
  85.1 0.0 copy-done.2
  85.1 0.7 copy.20
  85.8 0.0 copy-done.1
  85.8 0.7 copy.21
Async XLA Ops:
  80.5 3.3 %copy-start = (bf16[4096,128]{1,0:T(8,128)(2,1)S(1)}, bf16[4096,128]{1,0:T(8,128)(2,1)}, u32[]{:S(2)}) copy-start(bf16[4096,128]{1,0:T(8,128)(2,1)} %get-tuple-element.10) | copy-start | bytes 3145732
  83.8 1.3 %copy-start.2 = (bf16[512,128]{1,0:T(8,128)(2,1)S(1)}, bf16[512,128]{1,0:T(8,128)(2,1)}, u32[]{:S(2)}) copy-start(bf16[512,128]{1,0:T(8,128)(2,1)} %get-tuple-element.21) | copy-start | bytes 393220
  83.8 2.0 %copy-start.1 = (bf16[512,128]{1,0:T(8,128)(2,1)S(1)}, bf16[512,128]{1,0:T(8,128)(2,1)}, u32[]{:S(2)}) copy-start(bf16[512,128]{1,0:T(8,128)(2,1)} %get-tuple-element.22) | copy-start | bytes 393220

commit v2 on v1

--- a/solution.py
+++ b/solution.py
@@ -12,6 +12,7 @@
 F32 = jnp.float32
 BF16 = jnp.bfloat16
 VMEM = pl.BlockSpec(memory_space=pltpu.VMEM)
+CHAINS = 4
 SMEM = pl.BlockSpec(memory_space=pltpu.SMEM)
 
 
@@ -164,6 +165,25 @@
             def _():
                 self.copies[side].wait_send()
                 self.copies[1 - side].wait_recv()
+
+
+class Chain:
+    def __init__(self, at, length, order):
+        self.at, self.length, self.offset, self.order = at, length, at, order
+        self.places = []
+
+
+def finish_kernel(mixed, features, grads, *outs):
+    offsets = outs[2].shape[0]
+    width = mixed.shape[1]
+    outs[0][...] = mixed[...]
+    outs[1][...] = features[...]
+    outs[2][...] = grads[: offsets * width].astype(F32).reshape(outs[2].shape)
+    base = offsets * width
+    for j in range(outs[3].shape[1] // width):
+        outs[3][:, j * width : (j + 1) * width] = grads[base : base + width].astype(F32)
+        base += width
+    outs[4][...] = grads[base : base + width].astype(F32)
 
 
 def level_kernel(
@@ -281,41 +301,56 @@
     partial[: offsets * width] = dot(gathered[...], grad)
 
     bits = devices.bit_length() - 1
-    at, length, offset = 0, total_rows, 0
-    places = []
-
-    def halving(b, at, length, offset):
-        length = length // 2
+    orders = (list(range(bits)), list(range(1)) + list(range(2, bits)) + list(range(1, min(2, bits))))
+    share = total_rows // CHAINS
+    chains = [Chain(c * share, share, orders[c % 2]) for c in range(CHAINS)]
+
+    def halving(c, i):
+        chain = chains[c]
+        b = chain.order[i]
+        length = chain.length // 2
         bit = lax.rem(me // (1 << b), 2)
         other = me + (1 - 2 * bit) * (1 << b)
-        keep = pl.multiple_of(at + bit * length, 16)
-        give = pl.multiple_of(at + (1 - bit) * length, 16)
-        half_out[offset : offset + length] = partial[pl.ds(give, length)].astype(BF16)
-        copy = pltpu.make_async_remote_copy(
-            src_ref=half_out.at[pl.ds(offset, length)],
-            dst_ref=half_in.at[pl.ds(offset, length)],
-            send_sem=half_sems.at[2 * b],
-            recv_sem=half_sems.at[2 * b + 1],
+        keep = pl.multiple_of(chain.at + bit * length, 16)
+        give = pl.multiple_of(chain.at + (1 - bit) * length, 16)
+        part = pl.ds(chain.offset, length)
+        half_out[part] = partial[pl.ds(give, length)].astype(BF16)
+        chain.copy = pltpu.make_async_remote_copy(
+            src_ref=half_out.at[part],
+            dst_ref=half_in.at[part],
+            send_sem=half_sems.at[2 * (c * bits + i)],
+            recv_sem=half_sems.at[2 * (c * bits + i) + 1],
             device_id={"bricks": other},
             device_id_type=pl.DeviceIdType.MESH,
         )
-        copy.start()
-        return copy, keep, length
-
-    def doubling(b, at, length):
+        chain.copy.start()
+        chain.at, chain.length = keep, length
+        chain.places.append((keep, length))
+
+    def add_half(c):
+        chain = chains[c]
+        chain.copy.wait()
+        partial[pl.ds(chain.at, chain.length)] += half_in[
+            pl.ds(chain.offset, chain.length)
+        ].astype(F32)
+        chain.offset += chain.length
+
+    def doubling(c, i):
+        chain = chains[c]
+        b = chain.order[i]
+        at, length = chain.places[i]
         bit = lax.rem(me // (1 << b), 2)
         other = me + (1 - 2 * bit) * (1 << b)
         part = summed.at[pl.ds(pl.multiple_of(at, 16), length)]
-        copy = pltpu.make_async_remote_copy(
+        chain.copy = pltpu.make_async_remote_copy(
             src_ref=part,
             dst_ref=part,
-            send_sem=full_sems.at[2 * b],
-            recv_sem=full_sems.at[2 * b + 1],
+            send_sem=full_sems.at[2 * (c * bits + i)],
+            recv_sem=full_sems.at[2 * (c * bits + i) + 1],
             device_id={"bricks": other},
             device_id_type=pl.DeviceIdType.MESH,
         )
-        copy.start()
-        return copy
+        chain.copy.start()
 
     def contribution(k, carry):
         rows = pl.ds(pl.multiple_of(k * height, height), height)
@@ -347,21 +382,26 @@
     work += [functools.partial(own_rows, piece) for piece in range(height // 128)]
     work += [take_mixed, finish]
 
-    for b in range(bits):
-        copy, at, length = halving(b, at, length, offset)
-        places.append((at, length))
+    for c in range(CHAINS):
+        halving(c, 0)
+    for i in range(bits):
         if work:
             work.pop(0)()
-        copy.wait()
-        partial[pl.ds(at, length)] += half_in[offset : offset + length].astype(F32)
-        offset += length
-    summed[pl.ds(at, length)] = (partial[pl.ds(at, length)] * factor).astype(BF16)
-    for b in reversed(range(bits)):
-        at, length = places[b]
-        copy = doubling(b, at, length)
+        for c in range(CHAINS):
+            add_half(c)
+            if i + 1 < bits:
+                halving(c, i + 1)
+            else:
+                done = pl.ds(chains[c].at, chains[c].length)
+                summed[done] = (partial[done] * factor).astype(BF16)
+                doubling(c, bits - 1)
+    for i in reversed(range(bits)):
         if work:
             work.pop(0)()
-        copy.wait()
+        for c in range(CHAINS):
+            chains[c].copy.wait()
+            if i:
+                doubling(c, i - 1)
     for task in work:
         task()
     gathered_grads[...] = summed[...]
@@ -386,7 +426,7 @@
     slots = devices * cap
     parts = in_projection.shape[1] // width
     live = (offsets + parts + 1) * width
-    total_rows = -(-live // (16 * devices)) * 16 * devices
+    total_rows = -(-live // (16 * devices * CHAINS)) * 16 * devices * CHAINS
     bits = devices.bit_length() - 1
     factor = (height * devices) ** (-0.5)
     rows = pltpu.VMEM((devices, cap, width), BF16)
@@ -417,8 +457,8 @@
             pltpu.SemaphoreType.DMA((8,)),
             pltpu.SemaphoreType.DMA((4,)),
             pltpu.SemaphoreType.DMA((4,)),
-            pltpu.SemaphoreType.DMA((2 * bits,)),
-            pltpu.SemaphoreType.DMA((2 * bits,)),
+            pltpu.SemaphoreType.DMA((2 * bits * CHAINS,)),
+            pltpu.SemaphoreType.DMA((2 * bits * CHAINS,)),
         ],
         compiler_params=pltpu.CompilerParams(
             collective_id=0, has_side_effects=True, vmem_limit_bytes=56 * 1024 * 1024
@@ -435,9 +475,21 @@
         head_scale,
         send_count,
     )
-    grads = grads.astype(F32).reshape(-1, width, width)
-    grad_in = grads[offsets : offsets + parts].transpose(1, 0, 2).reshape(in_projection.shape)
-    return (mixed, grad_features, grads[:offsets], grad_in, grads[offsets + parts])
+    return tuple(
+        pl.pallas_call(
+            finish_kernel,
+            out_shape=(
+                shape((height, width), BF16),
+                shape((height, width), BF16),
+                shape(conv_weight.shape, F32),
+                shape(in_projection.shape, F32),
+                shape(out_projection.shape, F32),
+            ),
+            in_specs=[VMEM] * 3,
+            out_specs=[VMEM] * 5,
+            compiler_params=pltpu.CompilerParams(vmem_limit_bytes=32 * 1024 * 1024),
+        )(mixed, grad_features, grads)
+    )
 
 
 def solution(mesh):

time: 87.4 us -> 79.1 us (0.905)
  Pallas kernels: 78.6 us -> 73.9 us
  local copies, waits for them, and re-layouts: 7.24 us -> 4.29 us
    pallas_call x1, Pallas kernels: 78.6 us -> 72.5 us  [body(): pl.pallas_call(functools.partial(level_kernel, devices, cap, halo, total_...]
    slice x4 -> x0, local copies, waits for them, and re-layouts: 3.84 us -> none  [the longest x1 1.48 us: body(): grads[offsets + parts]]
    pallas_call x0 -> x1, Pallas kernels: none -> 1.43 us  [body(): pl.pallas_call(finish_kernel, out_shape=(shape((height, width), BF16), sh...]
    unnamed x9 -> x6, local copies, waits for them, and re-layouts: 2.14 us -> 3.03 us
where the time goes in v2:
time: 79.1 us; the launch traced here: 78.9 us
  Pallas kernels  73.9 us (93%)
  local copies, waits for them, and re-layouts  4.29 us (5%)
    pallas_call x1, Pallas kernels, body(): pl.pallas_call(functools.partial(level_kernel, devices, cap, halo, total_...  72.5 us
    unnamed x6, local copies, waits for them, and re-layouts  3.03 us

profile of v2, /device:TPU:0, one launch (start us, length us, event | category | flops | bytes accessed | tf_op | source)
XLA Modules:
  0.0 78.9 jit_solution(14020993188682936673)
XLA Ops:
  0.6 1.3 %reshape.20.send = s32[1,128]{1,0:T(1,128)} reshape(s32[2,64]{1,0:T(2,128)} %param.16) | data formatting | bytes 1024 | tf_op jit(solution)/shard_map/reshape | solution.py:472
  1.9 72.5 %shard_map.137 = (bf16[512,128]{1,0:T(8,128)(2,1)}, bf16[512,128]{1,0:T(8,128)(2,1)}, bf16[4096,128]{1,0:T(8,128)(2,1)}) custom-call(bf16[512,128]{1,0:T(8,128)(2,1)} %feat.1, bf16[3456,128]{1,0:T(8,128)(2,1)} %bitcast.2, bf16[128,384]{1,0:T(8,128)(2,1)} %in_proj.1, bf16[128,128]{1,0:T(8,128)(2,1)} %out_proj.1, s32[27,512]{1,0:T(8,128)} %near.1, ...), custom_call_target="tpu_custom_call" | custom-call | tf_op jit(solution)/shard_map/pallas_call | solution.py:435
  74.4 0.0 copy-start
  74.4 1.2 %copy-done = bf16[4096,128]{1,0:T(8,128)(2,1)S(1)} copy-done((bf16[4096,128]{1,0:T(8,128)(2,1)S(1)}, bf16[4096,128]{1,0:T(8,128)(2,1)}, u32[]{:S(2)}) %copy-start) | copy-done | bytes 1048600
  75.6 0.0 copy-start.1
  75.6 0.9 %copy-done.1 = bf16[512,128]{1,0:T(8,128)(2,1)S(1)} copy-done((bf16[512,128]{1,0:T(8,128)(2,1)S(1)}, bf16[512,128]{1,0:T(8,128)(2,1)}, u32[]{:S(2)}) %copy-start.1) | copy-done | bytes 131096
  76.5 0.0 copy-start.2
  76.5 0.9 %copy-done.2 = bf16[512,128]{1,0:T(8,128)(2,1)S(1)} copy-done((bf16[512,128]{1,0:T(8,128)(2,1)S(1)}, bf16[512,128]{1,0:T(8,128)(2,1)}, u32[]{:S(2)}) %copy-start.2) | copy-done | bytes 131096
  77.4 1.4 %shard_map.138 = (bf16[512,128]{1,0:T(8,128)(2,1)}, bf16[512,128]{1,0:T(8,128)(2,1)}, f32[27,128,128]{2,1,0:T(8,128)}, f32[128,384]{1,0:T(8,128)}, f32[128,128]{1,0:T(8,128)}) custom-call(bf16[512,128]{1,0:T(8,128)(2,1)S(1)} %copy-done.1, bf16[512,128]{1,0:T(8,128)(2,1)S(1)} %copy-done.2, bf16[4096,128]{1,0:T(8,128)(2,1)S(1)} %copy-done), custom_call_target="tpu_custom_call" | custom-call | tf_op jit(solution)/shard_map/pallas_call | solution.py:479
Async XLA Ops:
  74.4 1.2 %copy-start = (bf16[4096,128]{1,0:T(8,128)(2,1)S(1)}, bf16[4096,128]{1,0:T(8,128)(2,1)}, u32[]{:S(2)}) copy-start(bf16[4096,128]{1,0:T(8,128)(2,1)} %get-tuple-element.10.grads) | copy-start | bytes 3145732
  75.6 0.9 %copy-start.1 = (bf16[512,128]{1,0:T(8,128)(2,1)S(1)}, bf16[512,128]{1,0:T(8,128)(2,1)}, u32[]{:S(2)}) copy-start(bf16[512,128]{1,0:T(8,128)(2,1)} %get-tuple-element.8.mixed) | copy-start | bytes 393220
  76.5 0.9 %copy-start.2 = (bf16[512,128]{1,0:T(8,128)(2,1)S(1)}, bf16[512,128]{1,0:T(8,128)(2,1)}, u32[]{:S(2)}) copy-start(bf16[512,128]{1,0:T(8,128)(2,1)} %get-tuple-element.9.features) | copy-start | bytes 393220

commit v3 on v2

--- a/solution.py
+++ b/solution.py
@@ -173,24 +173,24 @@
         self.places = []
 
 
-def finish_kernel(mixed, features, grads, *outs):
+def finish_kernel(result, *outs):
     offsets = outs[2].shape[0]
-    width = mixed.shape[1]
-    outs[0][...] = mixed[...]
-    outs[1][...] = features[...]
-    outs[2][...] = grads[: offsets * width].astype(F32).reshape(outs[2].shape)
-    base = offsets * width
+    height, width = outs[0].shape
+    outs[0][...] = result[:height]
+    outs[1][...] = result[height : 2 * height]
+    base = 2 * height + offsets * width
+    outs[2][...] = result[2 * height : base].astype(F32).reshape(outs[2].shape)
     for j in range(outs[3].shape[1] // width):
-        outs[3][:, j * width : (j + 1) * width] = grads[base : base + width].astype(F32)
+        outs[3][:, j * width : (j + 1) * width] = result[base : base + width].astype(F32)
         base += width
-    outs[4][...] = grads[base : base + width].astype(F32)
+    outs[4][...] = result[base : base + width].astype(F32)
 
 
 def level_kernel(
     devices, cap, halo, total_rows, factor,
-    feat, weight, in_proj, out_proj, near, send, slot, cot, scale, count,
-    mixed, grad_features, gathered_grads,
-    stage, chosen, gathered, contrib, filtered, local, partial, summed,
+    feat, weight_hbm, in_proj, out_proj, near, send, slot, cot, scale, count,
+    result,
+    weight, weight_sem, stage, chosen, gathered, contrib, filtered, local, partial, summed,
     cot_out, cot_in, act_out, act_in, back_out, back_in, mix_out, mix_in,
     halo_out, halo_in, edge_out, edge_in, half_out, half_in,
     sems, halo_sems, edge_sems, half_sems, full_sems,
@@ -204,6 +204,8 @@
     barrier = pltpu.get_barrier_semaphore()
     halos = Edges(devices, me, halo_out, halo_in, halo_sems)
     edges = Edges(devices, me, edge_out, edge_in, edge_sems)
+    load = pltpu.make_async_copy(weight_hbm, weight, weight_sem)
+    load.start()
     halos.blank()
     edges.blank()
 
@@ -256,6 +258,7 @@
         return carry
 
     lax.fori_loop(0, offsets, gather, 0)
+    load.wait()
     total = dot(weight[...], gathered[...], 0, 0)
     filtered[...] = total
     activated = (total * jax.nn.sigmoid(total)).astype(BF16)
@@ -371,12 +374,12 @@
 
     def take_mixed():
         mixes.wait_recv()
-        mixed[...] = dot(mix_in[...].reshape(slots, width), to_slots, 0, 0).T.astype(BF16)
+        result[:height] = dot(mix_in[...].reshape(slots, width), to_slots, 0, 0).T.astype(BF16)
 
     def finish():
         edges.wait()
         returned = edge_in[...].reshape(2 * halo, width)
-        grad_features[...] = (local[...] + dot(border, returned)).astype(BF16)
+        result[height : 2 * height] = (local[...] + dot(border, returned)).astype(BF16)
 
     work = [edge_rows]
     work += [functools.partial(own_rows, piece) for piece in range(height // 128)]
@@ -404,7 +407,7 @@
                 doubling(c, i - 1)
     for task in work:
         task()
-    gathered_grads[...] = summed[...]
+    result[2 * height :] = summed[...]
     for other in (cots, acts, backs, mixes):
         other.wait_send()
 
@@ -432,16 +435,14 @@
     rows = pltpu.VMEM((devices, cap, width), BF16)
     marked = pltpu.VMEM((devices, cap + 16, width), BF16)
     pair = pltpu.VMEM((2, halo, width), BF16)
-    mixed, grad_features, grads = pl.pallas_call(
+    result = pl.pallas_call(
         functools.partial(level_kernel, devices, cap, halo, total_rows, factor),
-        out_shape=(
-            shape((height, width), BF16),
-            shape((height, width), BF16),
-            shape((total_rows, width), BF16),
-        ),
-        in_specs=[VMEM] * 8 + [SMEM] * 2,
-        out_specs=[VMEM] * 3,
+        out_shape=shape((2 * height + total_rows, width), BF16),
+        in_specs=[VMEM, pl.BlockSpec(memory_space=pl.ANY)] + [VMEM] * 6 + [SMEM] * 2,
+        out_specs=VMEM,
         scratch_shapes=[
+            pltpu.VMEM((offsets * width, width), BF16),
+            pltpu.SemaphoreType.DMA,
             pltpu.VMEM((devices, 16, 128), F32),
             pltpu.VMEM((height + 2 * halo, offsets * height), BF16),
             pltpu.VMEM((offsets * width, height), BF16),
@@ -485,10 +486,10 @@
                 shape(in_projection.shape, F32),
                 shape(out_projection.shape, F32),
             ),
-            in_specs=[VMEM] * 3,
+            in_specs=[VMEM],
             out_specs=[VMEM] * 5,
             compiler_params=pltpu.CompilerParams(vmem_limit_bytes=32 * 1024 * 1024),
-        )(mixed, grad_features, grads)
+        )(result)
     )
 
 

time: 79.1 us -> 77.2 us (0.976)
  local copies, waits for them, and re-layouts: 4.29 us -> 2.58 us
    unnamed x6 -> x2, local copies, waits for them, and re-layouts: 3.03 us -> 1.31 us
where the time goes in v3:
time: 77.2 us; the launch traced here: 77 us
  Pallas kernels  73.7 us (95%)
  local copies, waits for them, and re-layouts  2.58 us (3%)
    pallas_call x1, Pallas kernels, body(): pl.pallas_call(functools.partial(level_kernel, devices, cap, halo, total_...  72.3 us

profile of v3, /device:TPU:0, one launch (start us, length us, event | category | flops | bytes accessed | tf_op | source)
XLA Modules:
  0.0 77.0 jit_solution(13018616797297555910)
XLA Ops:
  0.6 1.3 %reshape.20.send = s32[1,128]{1,0:T(1,128)} reshape(s32[2,64]{1,0:T(2,128)} %param.16) | data formatting | bytes 1024 | tf_op jit(solution)/shard_map/reshape | solution.py:473
  1.9 72.3 %shard_map.137.result = bf16[5120,128]{1,0:T(8,128)(2,1)} custom-call(bf16[512,128]{1,0:T(8,128)(2,1)} %feat.1, bf16[3456,128]{1,0:T(8,128)(2,1)} %bitcast.2, bf16[128,384]{1,0:T(8,128)(2,1)} %in_proj.1, bf16[128,128]{1,0:T(8,128)(2,1)} %out_proj.1, s32[27,512]{1,0:T(8,128)} %near.1, s32[1,128]{1,0:T(1,128)} %reshape.20.send, s32[1,512]{1,0:T(1,128)} %bitcast.3, ...), custom_call_target="tpu_custom_call" | custom-call | tf_op jit(solution)/shard_map/pallas_call | solution.py:438
  74.2 0.0 copy-start
  74.2 1.3 %copy-done = bf16[5120,128]{1,0:T(8,128)(2,1)S(1)} copy-done((bf16[5120,128]{1,0:T(8,128)(2,1)S(1)}, bf16[5120,128]{1,0:T(8,128)(2,1)}, u32[]{:S(2)}) %copy-start) | copy-done | bytes 1310744
  75.5 1.4 %shard_map.138 = (bf16[512,128]{1,0:T(8,128)(2,1)}, bf16[512,128]{1,0:T(8,128)(2,1)}, f32[27,128,128]{2,1,0:T(8,128)}, f32[128,384]{1,0:T(8,128)}, f32[128,128]{1,0:T(8,128)}) custom-call(bf16[5120,128]{1,0:T(8,128)(2,1)S(1)} %copy-done), custom_call_target="tpu_custom_call" | custom-call | tf_op jit(solution)/shard_map/pallas_call | solution.py:480
Async XLA Ops:
  74.2 1.3 %copy-start = (bf16[5120,128]{1,0:T(8,128)(2,1)S(1)}, bf16[5120,128]{1,0:T(8,128)(2,1)}, u32[]{:S(2)}) copy-start(bf16[5120,128]{1,0:T(8,128)(2,1)} %shard_map.137.result) | copy-start | bytes 3932164
